TPU v7x, 32 devices: a whole 2x2x4 slice. The times are simulated.
32 devices in a mesh: groups: 2 (over x), dp: 16 (over z, y, core).
Axes of the slice: x: 2, y: 2, z: 4, core: 2. Of those that a mesh axis runs over, the one named last changes fastest.
Arguments:
- inputs: bfloat16 [4096, 8192], P(('groups', 'dp')), parts along dimension 0, may hold values from -6 to 6
- output_gradient: bfloat16 [4096, 1024], P(('groups', 'dp')), parts along dimension 0, may hold values from -6 to 6
- token_adapter_index: int32 [4096, 1], P(('groups', 'dp')), parts along dimension 0, may hold values from 0 to 15; in each aligned block of 128 rows (0 to 127, 128 to 255, ...) at most 12 rows name the same one
- owner_index_map: int32 [16], replicated, may hold values from 0 to 15, each once
- frozen_key_weight: bfloat16 [8192, 1024], P('dp'), may hold values from -0.0625 to 0.0625
- down_panels: bfloat16 [16, 8192, 64], P('dp'), may hold values from -0.0625 to 0.0625
- up_panels: bfloat16 [16, 64, 1024], P('dp'), may hold values from -0.1875 to 0.1875
Outputs:
- input_gradient: bfloat16 [4096, 8192], P(('groups', 'dp')), parts along dimension 0
- down_panel_gradient: float32 [32, 8192, 64], P(('groups', 'dp')), parts along dimension 0
- up_panel_gradient: float32 [32, 64, 1024], P(('groups', 'dp')), parts along dimension 0
There are 2 independent parts, one for each index of `groups`. A program takes and returns all parts, laid end to end along the dimension named above; an argument that names none is the same for every part. Nothing has to cross between parts.
Inputs may be any that keep to these rules, and one draw needn't show every extreme that they name: `token_adapter_index`: within the rows of one index of dp no adapter appears more than 12 times, and some adapter appears exactly 12 times there. `owner_index_map`: every index of dp owns exactly one adapter.
All inputs are finite; a program needn't handle non-finite values.
Results may differ from a plain program's by a relative error of at most 0.0042.
Values may be sent and summed in bfloat16 or wider, within the bound.
A program may use at most 128 MiB of HBM per device.

v0:
```python
import jax
import jax.numpy as jnp
from jax import lax
from jax.sharding import PartitionSpec as P

adapter_scale = 2.0


def frozen_part(output_gradient, frozen_key_weight):
    full_weight = lax.all_gather(frozen_key_weight, "dp", axis=0, tiled=True)
    return jnp.dot(output_gradient, full_weight.T, preferred_element_type=jnp.float32)


def adapter_term(
    inputs, output_gradient, token_adapter_index, owner_index_map, down_panels, up_panels
):
    token_count = lax.axis_size("dp")
    tok_rows = inputs.shape[0]
    adapter_list = down_panels.shape[0] * token_count
    slot_index = max(2, 3 * tok_rows // (2 * adapter_list))
    adapter_index = token_adapter_index[:, 0]
    onehot = (adapter_index[:, None] == jnp.arange(adapter_list, dtype=jnp.int32)[None, :]).astype(
        jnp.int32
    )
    rank_in = jnp.sum(onehot * (jnp.cumsum(onehot, axis=0) - 1), axis=1)
    target = owner_index_map[adapter_index] * slot_index + rank_in
    placement_rows = (
        jnp.arange(token_count * slot_index, dtype=jnp.int32)[:, None] == target[None, :]
    ).astype(jnp.bfloat16)
    send_x = jnp.dot(placement_rows, inputs, preferred_element_type=jnp.float32).astype(
        jnp.bfloat16
    )
    send_dy = jnp.dot(placement_rows, output_gradient, preferred_element_type=jnp.float32).astype(
        jnp.bfloat16
    )
    send_x = send_x.reshape(token_count, slot_index, inputs.shape[1])
    send_dy = send_dy.reshape(token_count, slot_index, output_gradient.shape[1])
    recv_x, recv_dy = (
        lax.all_to_all(send_x, "dp", split_axis=0, concat_axis=0, tiled=True),
        lax.all_to_all(send_dy, "dp", split_axis=0, concat_axis=0, tiled=True),
    )
    input_rows = recv_x.reshape(token_count * slot_index, inputs.shape[1])
    gradient_rows = recv_dy.reshape(token_count * slot_index, output_gradient.shape[1])
    down_panel = down_panels[0]
    up_panel = up_panels[0]
    hidden_state = jnp.dot(input_rows, down_panel, preferred_element_type=jnp.float32).astype(
        jnp.bfloat16
    )
    contract_rows = (((0,), (0,)), ((), ()))
    up_gradient_local = adapter_scale * lax.dot_general(
        hidden_state, gradient_rows, contract_rows, preferred_element_type=jnp.float32
    )
    adapter_gradient = (
        adapter_scale
        * lax.dot_general(
            gradient_rows, up_panel, (((1,), (1,)), ((), ())), preferred_element_type=jnp.float32
        )
    ).astype(jnp.bfloat16)
    down_gradient_local = lax.dot_general(
        input_rows, adapter_gradient, contract_rows, preferred_element_type=jnp.float32
    )
    adapter_input = lax.dot_general(
        adapter_gradient, down_panel, (((1,), (1,)), ((), ())), preferred_element_type=jnp.float32
    ).astype(jnp.bfloat16)
    returned_rows = lax.all_to_all(
        adapter_input.reshape(token_count, slot_index, inputs.shape[1]),
        "dp",
        split_axis=0,
        concat_axis=0,
        tiled=True,
    )
    returned_rows = returned_rows.reshape(token_count * slot_index, inputs.shape[1])
    adapter_tokens = lax.dot_general(
        placement_rows, returned_rows, contract_rows, preferred_element_type=jnp.float32
    )
    return (adapter_tokens, down_gradient_local[None], up_gradient_local[None])


def per_device(
    inputs,
    output_gradient,
    token_adapter_index,
    owner_index_map,
    frozen_key_weight,
    down_panels,
    up_panels,
):
    base_term = frozen_part(output_gradient, frozen_key_weight)
    adapter_tokens, down_panel_gradient, up_panel_gradient = adapter_term(
        inputs, output_gradient, token_adapter_index, owner_index_map, down_panels, up_panels
    )
    input_gradient = (base_term + adapter_tokens).astype(jnp.bfloat16)
    return (input_gradient, down_panel_gradient, up_panel_gradient)


def solution(mesh):
    in_specs = (
        P(("groups", "dp"), None),
        P(("groups", "dp"), None),
        P(("groups", "dp"), None),
        P(),
        P("dp", None),
        P("dp", None, None),
        P("dp", None, None),
    )
    out_specs = (
        P(("groups", "dp"), None),
        P(("groups", "dp"), None, None),
        P(("groups", "dp"), None, None),
    )
    return jax.shard_map(
        per_device, mesh=mesh, in_specs=in_specs, out_specs=out_specs, check_vma=False
    )
```

profile of v0, /device:TPU:15, one launch (start us, length us, event | category | flops | bytes accessed | tf_op | source)
XLA Modules:
  0.0 353.1 jit_solution(7832417390575793770)
XLA Ops:
  7.9 0.7 fusion.8
  8.8 2.0 fusion.15
  10.8 0.8 select_reduce_fusion
  11.6 10.6 %fusion.14 = s32[128]{0:T(128)S(1)} fusion(s32[128]{0:T(128)S(1)} %select_reduce_fusion, s32[128,1]{0,1:T(1,128)} %param.9, s32[]{:T(128)} %bitcast.18, s32[]{:T(128)} %bitcast.19, s32[]{:T(128)} %bitcast.20, s32[]{:T(128)} %bitcast.21, s32[]{:T(128)} %bitcast.22, s32[]{:T(128)} %bitcast.24, s32[]{:T(128)} %bitcast.23, s32[]{:T(128)} %bitcast.1, s32[]{:T(128)} %bitcast.3, ...), kind=kLoop, calls=%fused_computation.39 | loop fusion | flops 4480 | bytes 1600 | tf_op jit(solution)/shard_map/add | solution.py:26
  22.2 1.2 convolution_convert_fusion.2
  23.4 0.9 reshape.30
  24.3 6.6 %all-to-all-start = ((bf16[16,12,1024]{2,1,0:T(8,128)(2,1)}), bf16[16,12,1024]{2,1,0:T(8,128)(2,1)}, u32[]{:S(2)}, u32[]{:S(2)}) async-start(bf16[16,12,1024]{2,1,0:T(8,128)(2,1)} %reshape.30), calls=%async_computation | async-start | bytes 1048576 | tf_op jit(solution)/shard_map/all_to_all | solution.py:40
  30.9 2.6 convolution_convert_fusion
  33.5 4.8 %reshape.34 = bf16[16,12,8192]{2,1,0:T(8,128)(2,1)} reshape(bf16[192,8192]{1,0:T(8,128)(2,1)} %convolution_convert_fusion) | data formatting | bytes 6291456 | tf_op jit(solution)/shard_map/reshape | solution.py:36
  38.2 20.1 %all-to-all-done = bf16[16,12,1024]{2,1,0:T(8,128)(2,1)} async-done(((bf16[16,12,1024]{2,1,0:T(8,128)(2,1)}), bf16[16,12,1024]{2,1,0:T(8,128)(2,1)}, u32[]{:S(2)}, u32[]{:S(2)}) %all-to-all-start) | async-done | bytes 393248 | tf_op jit(solution)/shard_map/all_to_all | solution.py:40
  58.3 5.5 %all-to-all-start.2 = ((bf16[16,12,8192]{2,1,0:T(8,128)(2,1)}), bf16[16,12,8192]{2,1,0:T(8,128)(2,1)}, u32[]{:S(2)}, u32[]{:S(2)}) async-start(bf16[16,12,8192]{2,1,0:T(8,128)(2,1)} %reshape.34), calls=%async_computation.2 | async-start | bytes 8388608 | tf_op jit(solution)/shard_map/all_to_all | solution.py:39
  63.8 1.1 reshape.31
  65.0 1.2 fusion.2
  66.7 2.6 convolution_convert_fusion.1
  69.4 4.7 %reshape.32 = bf16[16,12,8192]{2,1,0:T(8,128)(2,1)} reshape(bf16[192,8192]{1,0:T(8,128)(2,1)} %convolution_convert_fusion.1) | data formatting | bytes 6291456 | tf_op jit(solution)/shard_map/reshape | solution.py:66
  74.1 152.0 %all-to-all-done.2 = bf16[16,12,8192]{2,1,0:T(8,128)(2,1)} async-done(((bf16[16,12,8192]{2,1,0:T(8,128)(2,1)}), bf16[16,12,8192]{2,1,0:T(8,128)(2,1)}, u32[]{:S(2)}, u32[]{:S(2)}) %all-to-all-start.2) | async-done | bytes 3145760 | tf_op jit(solution)/shard_map/all_to_all | solution.py:39
  226.0 4.5 %all-to-all-start.1 = ((bf16[16,12,8192]{2,1,0:T(8,128)(2,1)}), bf16[16,12,8192]{2,1,0:T(8,128)(2,1)}, u32[]{:S(2)}, u32[]{:S(2)}) async-start(bf16[16,12,8192]{2,1,0:T(8,128)(2,1)} %reshape.32), calls=%async_computation.1 | async-start | bytes 8388608 | tf_op jit(solution)/shard_map/all_to_all | solution.py:65
  230.6 4.8 %reshape.35 = bf16[192,8192]{1,0:T(8,128)(2,1)} reshape(bf16[16,12,8192]{2,1,0:T(8,128)(2,1)} %all-to-all-done.2) | data formatting | bytes 6291456 | tf_op jit(solution)/shard_map/reshape | solution.py:42
  235.3 3.9 %convolution_bitcast_fusion = f32[1,8192,64]{1,2,0:T(8,128)} fusion(bf16[192,64]{0,1:T(8,128)(2,1)} %copy-done.3, bf16[192,8192]{1,0:T(8,128)(2,1)} %reshape.35), kind=kOutput, calls=%fused_computation.4 | convolution fusion | flops 201326592 | bytes 5267456 | tf_op jit(solution)/shard_map/dot_general | solution.py:59
  239.3 3.9 %fusion.1 = f32[1,64,1024]{2,1,0:T(8,128)} fusion(bf16[192,1024]{1,0:T(8,128)(2,1)S(1)} %reshape.31, bf16[192,8192]{1,0:T(8,128)(2,1)} %reshape.35, bf16[1,8192,64]{1,2,0:T(8,128)(2,1)S(1)} %copy-done.1), kind=kOutput, calls=%fused_computation.7 | convolution fusion | flops 226570240 | bytes 4849664 | tf_op jit(solution)/shard_map/dot_general | solution.py:50
  243.1 79.9 %all-to-all-done.1 = bf16[16,12,8192]{2,1,0:T(8,128)(2,1)} async-done(((bf16[16,12,8192]{2,1,0:T(8,128)(2,1)}), bf16[16,12,8192]{2,1,0:T(8,128)(2,1)}, u32[]{:S(2)}, u32[]{:S(2)}) %all-to-all-start.1) | async-done | bytes 3145760 | tf_op jit(solution)/shard_map/all_to_all | solution.py:65
  323.0 4.7 %reshape.33 = bf16[192,8192]{1,0:T(8,128)(2,1)} reshape(bf16[16,12,8192]{2,1,0:T(8,128)(2,1)} %all-to-all-done.1) | data formatting | bytes 6291456 | tf_op jit(solution)/shard_map/reshape | solution.py:72
  327.8 13.2 %fusion.16 = f32[128,8192]{1,0:T(8,128)} fusion(bf16[128,1024]{1,0:T(8,128)(2,1)S(1)} %copy-done.2, bf16[8192,1024]{1,0:T(8,128)(2,1)} %all-gather.2.cloned.1.call-done), kind=kOutput, calls=%fused_computation.41 | convolution fusion | flops 2147483648 | bytes 21233664 | tf_op jit(solution)/shard_map/dot_general | solution.py:11
  341.0 5.2 %fusion = bf16[128,8192]{1,0:T(8,128)(2,1)} fusion(f32[128,8192]{1,0:T(8,128)} %fusion.16, bf16[192,8192]{1,0:T(8,128)(2,1)} %reshape.33, s32[128]{0:T(128)S(1)} %fusion.14), kind=kOutput, calls=%fused_computation.3 | convolution fusion | flops 404774912 | bytes 9437696 | tf_op jit(solution)/shard_map/dot_general | solution.py:73
  (12 shorter events, 1.5 us)
Async XLA Ops:
  7.2 23.7 %copy-start = (bf16[128,8192]{1,0:T(8,128)(2,1)S(1)}, bf16[128,8192]{1,0:T(8,128)(2,1)}, u32[]{:S(2)}) copy-start(bf16[128,8192]{1,0:T(8,128)(2,1)} %param.7) | copy-start | bytes 6291460
  7.2 320.6 %all-gather.2.cloned.1.call-start = ((), (), s32[]{:S(2)}) async-start(), calls=%async_computation.3 | async-start | bytes 17825792 | tf_op jit(solution)/shard_map/all_gather | solution.py:10
  24.3 34.0 %all-to-all-start = ((bf16[16,12,1024]{2,1,0:T(8,128)(2,1)}), bf16[16,12,1024]{2,1,0:T(8,128)(2,1)}, u32[]{:S(2)}, u32[]{:S(2)}) async-start(bf16[16,12,1024]{2,1,0:T(8,128)(2,1)} %reshape.30), calls=%async_computation | async-start | bytes 1048576 | tf_op jit(solution)/shard_map/all_to_all | solution.py:40
  38.2 28.5 %copy-start.1 = (bf16[1,8192,64]{1,2,0:T(8,128)(2,1)S(1)}, bf16[1,8192,64]{1,2,0:T(8,128)(2,1)}, u32[]{:S(2)}) copy-start(bf16[1,8192,64]{1,2,0:T(8,128)(2,1)} %param.12) | copy-start | bytes 3145732
  58.3 167.7 %all-to-all-start.2 = ((bf16[16,12,8192]{2,1,0:T(8,128)(2,1)}), bf16[16,12,8192]{2,1,0:T(8,128)(2,1)}, u32[]{:S(2)}, u32[]{:S(2)}) async-start(bf16[16,12,8192]{2,1,0:T(8,128)(2,1)} %reshape.34), calls=%async_computation.2 | async-start | bytes 8388608 | tf_op jit(solution)/shard_map/all_to_all | solution.py:39
  66.1 0.6 copy-start.3
  226.0 97.0 %all-to-all-start.1 = ((bf16[16,12,8192]{2,1,0:T(8,128)(2,1)}), bf16[16,12,8192]{2,1,0:T(8,128)(2,1)}, u32[]{:S(2)}, u32[]{:S(2)}) async-start(bf16[16,12,8192]{2,1,0:T(8,128)(2,1)} %reshape.32), calls=%async_computation.1 | async-start | bytes 8388608 | tf_op jit(solution)/shard_map/all_to_all | solution.py:65
  243.1 84.6 %copy-start.2 = (bf16[128,1024]{1,0:T(8,128)(2,1)S(1)}, bf16[128,1024]{1,0:T(8,128)(2,1)}, u32[]{:S(2)}) copy-start(bf16[128,1024]{1,0:T(8,128)(2,1)} %param.8) | copy-start | bytes 786436
Sparse Core Ops, SparseCore 0:
  10.2 211.0 all-gather.1
where the time goes:
time: 354 us; the launch traced here: 353 us
  waiting for transfers between devices  253 us (71%)
  matrix products  33.9 us (10%)
  local copies, waits for them, and re-layouts  23.5 us (7%)
  starting transfers between devices  16.7 us (5%)
  between operations  14.1 us (4%)
  other arithmetic  12.3 us (3%)
    all_to_all x1, waiting for transfers between devices, adapter_term(): lax.all_to_all(send_x, 'dp', split_axis=0, concat_axis=0, tiled=True)  152 us
    all_to_all x1, waiting for transfers between devices, adapter_term(): lax.all_to_all(adapter_input.reshape(token_count, slot_index, inputs.shap...  79.9 us
    all_to_all x1, waiting for transfers between devices, adapter_term(): lax.all_to_all(send_dy, 'dp', split_axis=0, concat_axis=0, tiled=True)  20.1 us
    dot_general x1, matrix products, frozen_part(): jnp.dot(output_gradient, full_weight.T, preferred_element_type=jnp.float32)  13.2 us
    add x1, other arithmetic, adapter_term(): target = owner_index_map[adapter_index] * slot_index + rank_in  10.6 us
  transfers between devices with their start and end apart: 4, of which 3 were waited for; matrix products, arithmetic and copies ran while one was open for 14% of the time, Pallas kernels for 0%

commit v1 on v0

v1 whole, which is shorter than its diff:
```python
import functools

import jax
import jax.numpy as jnp
from jax import lax
from jax.experimental import pallas as pl
from jax.experimental.pallas import tpu as pltpu
from jax.sharding import PartitionSpec as P

adapter_scale = 2.0
MESH = pl.DeviceIdType.MESH
ROWS = 16


def exchange_kernel(
    G,
    S,
    N,
    rank,
    x_ref,
    dyr_ref,
    dy_ref,
    w_ref,
    pt_ref,
    place_ref,
    hot_ref,
    q_ref,
    out_ref,
    rx_ref,
    rdy_out,
    lg_out,
    rdy,
    lg,
    rlg,
    wsh,
    psh,
    dyp,
    tiles,
    osend,
    expand,
    local_sem,
    dy_s,
    dy_r,
    lg_s,
    lg_r,
    p_s,
    p_r,
    x_s,
    x_r,
    w_s,
    w_r,
    b_s,
    b_r,
    t_s,
    t_r,
    o_s,
    o_r,
):
    PL = G * S
    L = N // S
    RG = w_ref.shape[0] // G
    T = dy_ref.shape[0]
    me_g = lax.axis_index("groups")
    me = lax.axis_index("dp")
    me_z = me // S
    me_s = lax.rem(me, S)
    me_p = me_g * S + me_s

    def group_dev(k):
        return lax.rem(me + k, N)

    def group_src(k):
        return lax.rem(me + N - k, N)

    def plane_dev(k):
        p = lax.rem(me_p + k, PL)
        return (p // S, me_z * S + lax.rem(p, S)), p

    def line_dev(k):
        return (me_g, lax.rem(me_z + k, L) * S + me_s)

    def rcopy(src, dst, ss, rs, dev):
        return pltpu.make_async_remote_copy(
            src_ref=src, dst_ref=dst, send_sem=ss, recv_sem=rs, device_id=dev, device_id_type=MESH
        )

    def each(lo, hi, body):
        def step(k, c):
            body(k)
            return c

        lax.fori_loop(lo, hi, step, 0)

    barrier = pltpu.get_barrier_semaphore()
    each(
        1,
        N,
        lambda k: pl.semaphore_signal(
            barrier, inc=1, device_id=(me_g, group_dev(k)), device_id_type=MESH
        ),
    )
    others = (G - 1) * S

    def greet(k):
        gg = lax.rem(me_g + 1 + k // S, G)
        pl.semaphore_signal(
            barrier,
            inc=1,
            device_id=(gg, me_z * S + lax.rem(k, S)),
            device_id_type=MESH,
        )

    each(0, others, greet)
    pl.semaphore_wait(barrier, N - 1 + others)

    def dy_copy(k):
        d = group_dev(k)
        return rcopy(dyr_ref.at[d], rdy.at[me], dy_s.at[k], dy_r.at[k], (me_g, d))

    each(1, N, lambda k: dy_copy(k).start())
    own_dy = pltpu.make_async_copy(dyr_ref.at[me], rdy.at[me], local_sem.at[0])
    own_dy.start()

    def b_copy(k):
        dev, _ = plane_dev(k)
        return rcopy(dy_ref, dyp.at[me_p], b_s.at[k], b_r.at[k], dev)

    each(1, PL, lambda k: b_copy(k).start())
    own_b = pltpu.make_async_copy(dy_ref, dyp.at[me_p], local_sem.at[1])
    own_b.start()

    w_part = w_ref.at[pl.ds(pl.multiple_of(me_g * RG, RG), RG)]

    def w_copy(k):
        return rcopy(w_part, wsh.at[me_z], w_s.at[k], w_r.at[k], line_dev(k))

    each(1, L, lambda k: w_copy(k).start())
    own_w = pltpu.make_async_copy(w_part, wsh.at[me_z], local_sem.at[2])
    own_w.start()

    def p_copy(k):
        d = group_dev(k)
        return rcopy(pt_ref.at[lax.rem(d, S)], psh.at[me], p_s.at[k], p_r.at[k], (me_g, d))

    each(1, N, lambda k: p_copy(k).start())
    own_p = pltpu.make_async_copy(pt_ref.at[me_s], psh.at[me], local_sem.at[3])
    own_p.start()

    each(1, N, lambda k: dy_copy(k).wait_recv())
    own_dy.wait()
    value = adapter_scale * lax.dot_general(
        rdy[...].reshape(N * ROWS, rdy.shape[2]),
        q_ref[...],
        (((1,), (1,)), ((), ())),
        preferred_element_type=jnp.float32,
    )
    lg[...] = value.astype(jnp.bfloat16).reshape(lg.shape)

    def lg_copy(k):
        d = group_dev(k)
        return rcopy(lg.at[d], rlg.at[me], lg_s.at[k], lg_r.at[k], (me_g, d))

    each(1, N, lambda k: lg_copy(k).start())
    own_lg = pltpu.make_async_copy(lg.at[me], rlg.at[me], local_sem.at[4])
    own_lg.start()
    save_dy = pltpu.make_async_copy(rdy, rdy_out, local_sem.at[5])
    save_dy.start()
    save_lg = pltpu.make_async_copy(lg, lg_out, local_sem.at[6])
    save_lg.start()

    def x_copy(k):
        d = group_dev(k)
        return rcopy(x_ref.at[d], rx_ref.at[me], x_s.at[k], x_r.at[k], (me_g, d))

    each(1, N, lambda k: x_copy(k).start())
    own_x = pltpu.make_async_copy(x_ref.at[me], rx_ref.at[me], local_sem.at[7])
    own_x.start()

    TL = tiles.shape[2]
    row = lax.broadcasted_iota(jnp.int32, (TL, N * rank), 0)
    col = lax.broadcasted_iota(jnp.int32, (TL, N * rank), 1)
    expand[0] = jnp.where(row == lax.rem(col, rank), 1.0, 0.0).astype(jnp.bfloat16)
    expand[1] = jnp.where(row - rank == col // rank, 1.0, 0.0).astype(jnp.bfloat16)

    each(1, N, lambda k: lg_copy(k).wait_recv())
    own_lg.wait()
    tokens = jnp.dot(
        place_ref[...], rlg[...].reshape(N * ROWS, TL), preferred_element_type=jnp.float32
    )
    tiles[me_p] = tokens.astype(jnp.bfloat16) + hot_ref[...]

    def t_copy(k):
        dev, _ = plane_dev(k)
        return rcopy(tiles.at[me_p], tiles.at[me_p], t_s.at[k], t_r.at[k], dev)

    each(1, PL, lambda k: t_copy(k).start())
    each(1, PL, lambda k: b_copy(k).wait_recv())
    own_b.wait()
    each(1, L, lambda k: w_copy(k).wait_recv())
    own_w.wait()
    each(1, PL, lambda k: t_copy(k).wait_recv())
    each(1, N, lambda k: p_copy(k).wait_recv())
    own_p.wait()

    def o_copy(k):
        dev, p = plane_dev(k)
        return rcopy(osend.at[p], out_ref.at[me_p], o_s.at[k], o_r.at[k], dev)

    def block(k):
        p = lax.rem(me_p + k, PL)
        base = lax.dot_general(
            dyp[p],
            wsh[...].reshape(L * RG, wsh.shape[2]),
            (((1,), (1,)), ((), ())),
            preferred_element_type=jnp.float32,
        )
        tile = tiles[p]
        spread = jnp.dot(tile, expand[0], preferred_element_type=jnp.float32)
        chosen = jnp.dot(tile, expand[1], preferred_element_type=jnp.float32)
        masked = (spread * chosen).astype(jnp.bfloat16)
        term = jnp.dot(
            masked, psh[...].reshape(N * rank, psh.shape[2]), preferred_element_type=jnp.float32
        ).astype(jnp.bfloat16)
        osend[p] = (base + term.astype(jnp.float32)).astype(jnp.bfloat16)

    def block_and_send(k):
        block(k)
        o_copy(k).start()

    each(1, PL, block_and_send)
    block(0)
    own_o = pltpu.make_async_copy(osend.at[me_p], out_ref.at[me_p], local_sem.at[8])
    own_o.start()

    each(1, PL, lambda k: o_copy(k).wait_recv())
    each(1, N, lambda k: x_copy(k).wait_recv())
    own_x.wait()
    own_o.wait()
    save_dy.wait()
    save_lg.wait()
    each(1, N, lambda k: dy_copy(k).wait_send())
    each(1, N, lambda k: lg_copy(k).wait_send())
    each(1, N, lambda k: p_copy(k).wait_send())
    each(1, N, lambda k: x_copy(k).wait_send())
    each(1, L, lambda k: w_copy(k).wait_send())
    each(1, PL, lambda k: b_copy(k).wait_send())
    each(1, PL, lambda k: t_copy(k).wait_send())
    each(1, PL, lambda k: o_copy(k).wait_send())


def per_device(
    G,
    inputs,
    output_gradient,
    token_adapter_index,
    owner_index_map,
    frozen_key_weight,
    down_panels,
    up_panels,
):
    N = lax.axis_size("dp")
    S = max(1, 8 // G)
    L = N // S
    PL = G * S
    T, D = inputs.shape
    K = output_gradient.shape[1]
    R = frozen_key_weight.shape[0]
    RG = R // G
    rank = down_panels.shape[2]
    cap = max(2, 3 * T // (2 * N))
    TL = -(-(rank + N) // 128) * 128
    bf16 = jnp.bfloat16

    index = token_adapter_index[:, 0]
    hot = index[:, None] == jnp.arange(N, dtype=jnp.int32)[None, :]
    before = jnp.arange(T)[:, None] > jnp.arange(T)[None, :]
    earlier = jnp.dot(before.astype(bf16), hot.astype(bf16), preferred_element_type=jnp.float32)
    place_in = jnp.sum(jnp.where(hot, earlier, 0.0), axis=1).astype(jnp.int32)
    owner = jnp.sum(jnp.where(hot, owner_index_map[None, :], 0), axis=1)
    slots12 = (jnp.arange(N * cap, dtype=jnp.int32)[:, None] == (owner * cap + place_in)[None, :])
    slots16 = (jnp.arange(N * ROWS, dtype=jnp.int32)[:, None] == (owner * ROWS + place_in)[None, :])
    place_x = slots12.astype(bf16)
    place_dy = slots16.astype(bf16)
    place_t = (
        (owner * ROWS + place_in)[:, None] == jnp.arange(N * ROWS, dtype=jnp.int32)[None, :]
    ).astype(bf16)
    owner_hot = (owner[:, None] == jnp.arange(TL, dtype=jnp.int32)[None, :] - rank).astype(bf16)

    send_x = jnp.dot(place_x, inputs, preferred_element_type=jnp.float32).astype(bf16)
    send_x = send_x.reshape(N, cap * D // 512, 512)
    send_dy = jnp.dot(place_dy, output_gradient, preferred_element_type=jnp.float32).astype(bf16)
    send_dy = send_dy.reshape(N, ROWS, K)

    panel = down_panels[0]
    group = lax.axis_index("groups")
    mine = lax.dynamic_index_in_dim(panel.reshape(L, S, G, RG, rank), group, 2, keepdims=False)
    shares = mine.transpose(1, 3, 0, 2).reshape(S, rank, L * RG)
    up_panel = up_panels[0]
    up_padded = jnp.pad(up_panel, ((0, TL - rank), (0, 0)))

    anyspace = pl.BlockSpec(memory_space=pl.ANY)
    vmem = pl.BlockSpec(memory_space=pltpu.VMEM)
    dma = pltpu.SemaphoreType.DMA
    outs, rx, rdy, lg = pl.pallas_call(
        functools.partial(exchange_kernel, G, S, N, rank),
        out_shape=(
            jax.ShapeDtypeStruct((PL, T, L * RG), bf16),
            jax.ShapeDtypeStruct(send_x.shape, bf16),
            jax.ShapeDtypeStruct(send_dy.shape, bf16),
            jax.ShapeDtypeStruct((N, ROWS, TL), bf16),
        ),
        in_specs=[anyspace] * 5 + [vmem] * 3,
        out_specs=[anyspace] * 4,
        scratch_shapes=[
            pltpu.VMEM((N, ROWS, K), bf16),
            pltpu.VMEM((N, ROWS, TL), bf16),
            pltpu.VMEM((N, ROWS, TL), bf16),
            pltpu.VMEM((L, RG, K), bf16),
            pltpu.VMEM((N, rank, L * RG), bf16),
            pltpu.VMEM((PL, T, K), bf16),
            pltpu.VMEM((PL, T, TL), bf16),
            pltpu.VMEM((PL, T, L * RG), bf16),
            pltpu.VMEM((2, TL, N * rank), bf16),
            dma((9,)),
        ]
        + [dma((N,))] * 8
        + [dma((L,))] * 2
        + [dma((PL,))] * 6,
        compiler_params=pltpu.CompilerParams(
            collective_id=0, has_side_effects=True, vmem_limit_bytes=48 * 1024 * 1024
        ),
        cost_estimate=pl.CostEstimate(
            flops=4 * PL * T * L * RG * K, bytes_accessed=16 * 1024 * 1024, transcendentals=0
        ),
        name="exchange",
    )(send_x, send_dy, output_gradient, frozen_key_weight, shares, place_t, owner_hot, up_padded)

    input_gradient = (
        outs.reshape(G, S, T, L, RG).transpose(2, 3, 1, 0, 4).reshape(T, D)
    )
    rows = rx.reshape(N * cap, D)
    gradient_rows = rdy[:, :cap].reshape(N * cap, K)
    lora = lg[:, :cap, :rank].reshape(N * cap, rank)
    contract_rows = (((0,), (0,)), ((), ()))
    hidden = jnp.dot(rows, panel, preferred_element_type=jnp.float32).astype(bf16)
    up_gradient = adapter_scale * lax.dot_general(
        hidden, gradient_rows, contract_rows, preferred_element_type=jnp.float32
    )
    down_gradient = lax.dot_general(
        rows, lora, contract_rows, preferred_element_type=jnp.float32
    )
    return (input_gradient, down_gradient[None], up_gradient[None])


def solution(mesh):
    in_specs = (
        P(("groups", "dp"), None),
        P(("groups", "dp"), None),
        P(("groups", "dp"), None),
        P(),
        P("dp", None),
        P("dp", None, None),
        P("dp", None, None),
    )
    out_specs = (
        P(("groups", "dp"), None),
        P(("groups", "dp"), None, None),
        P(("groups", "dp"), None, None),
    )
    return jax.shard_map(
        functools.partial(per_device, mesh.shape["groups"]),
        mesh=mesh,
        in_specs=in_specs,
        out_specs=out_specs,
        check_vma=False,
    )
```

time: 354 us -> 253 us (0.71)
  the two profiles are of different devices: /device:TPU:15 before, /device:TPU:1 now
where the time goes in v1:
time: 253 us; the launch traced here: 250 us
  Pallas kernels  194 us (77%)
  local copies, waits for them, and re-layouts  40.3 us (16%)
  matrix products  12.5 us (5%)
    pallas_call x1, Pallas kernels, per_device(): pl.pallas_call(functools.partial(exchange_kernel, G, S, N, rank), out_sha...  194 us
    reshape x2, local copies, waits for them, and re-layouts, per_device(): outs.reshape(G, S, T, L, RG).transpose(2, 3, 1, 0, 4).reshape(T, D)  8.96 us
    transpose x1, local copies, waits for them, and re-layouts, per_device(): outs.reshape(G, S, T, L, RG).transpose(2, 3, 1, 0, 4).reshape(T, D)  6.14 us
    reshape x1, local copies, waits for them, and re-layouts, per_device(): rows = rx.reshape(N * cap, D)  5.94 us
    reshape x1, local copies, waits for them, and re-layouts, per_device(): send_x = send_x.reshape(N, cap * D // 512, 512)  5.85 us
    unnamed x14, local copies, waits for them, and re-layouts  5.3 us

profile of v1, /device:TPU:1, one launch (start us, length us, event | category | flops | bytes accessed | tf_op | source)
XLA Modules:
  0.0 249.7 jit_solution(14349280681982231823)
XLA Ops:
  0.6 0.9 select_reduce_fusion
  1.6 0.9 fusion.1
  2.5 0.7 compare_convert_fusion.hot_ref
  3.3 0.9 pad.4.q_ref
  4.2 1.2 convolution_convert_fusion.1
  5.4 2.6 %reshape_squeeze.3 = bf16[4,4,2,256,64]{3,2,1,0,4:T(2,128)(2,1)} reshape(bf16[1,8192,64]{1,2,0:T(8,128)(2,1)} %param.12) | data formatting | bytes 2097152 | tf_op jit(solution)/shard_map/reshape;squeeze | solution.py:296
  8.0 2.4 constant_dynamic-slice_fusion
  10.5 0.3 copy.15
  10.8 1.2 reshape.59.pt_ref
  11.9 2.6 %convolution_convert_fusion = bf16[192,8192]{1,0:T(8,128)(2,1)} fusion(bf16[128,8192]{1,0:T(8,128)(2,1)S(1)} %copy-done, s32[128]{0:T(128)S(1)} %get-tuple-element.12), kind=kOutput, calls=%fused_computation | convolution fusion | flops 404250624 | bytes 5243392 | tf_op jit(solution)/shard_map/dot_general | solution.py:289
  14.5 5.9 %reshape.57.x_ref = bf16[16,192,512]{2,1,0:T(8,128)(2,1)} reshape(bf16[192,8192]{1,0:T(8,128)(2,1)} %convolution_convert_fusion) | data formatting | bytes 6291456 | tf_op jit(solution)/shard_map/reshape | solution.py:290
  20.4 1.0 copy-done.2
  21.4 0.9 copy-done.3
  22.4 0.8 copy-done.4
  23.2 1.2 copy-done.5
  24.4 194.4 %exchange.1 = (bf16[8,128,1024]{2,1,0:T(8,128)(2,1)S(1)}, bf16[16,192,512]{2,1,0:T(8,128)(2,1)}, bf16[16,16,1024]{2,1,0:T(8,128)(2,1)S(1)}, bf16[16,16,128]{2,1,0:T(8,128)(2,1)S(1)}) custom-call(bf16[16,192,512]{2,1,0:T(8,128)(2,1)} %reshape.57.x_ref, bf16[16,16,1024]{2,1,0:T(8,128)(2,1)S(1)} %bitcast.29, bf16[128,1024]{1,0:T(8,128)(2,1)S(1)} %copy-done.3, ...), custom_call_target="tpu_custom_call" | custom-call | flops 4294967296 | bytes 16777216 | tf_op jit(solution)/shard_map/exchange/pallas_call | solution.py:304
  218.8 1.3 copy-done.1
  220.1 4.5 %reshape.60 = bf16[2,4,128,4,256]{4,3,2,1,0:T(4,128)(2,1)} reshape(bf16[8,128,1024]{2,1,0:T(8,128)(2,1)} %copy-done.1) | data formatting | bytes 4194304 | tf_op jit(solution)/shard_map/reshape | solution.py:339
  224.6 6.1 %copy.13 = bf16[128,4,4,2,256]{4,3,2,1,0:T(2,128)(2,1)} copy(bf16[128,4,4,2,256]{4,1,0,2,3:T(4,128)(2,1)} %bitcast.31) | data formatting | bytes 4194304 | tf_op jit(solution)/shard_map/transpose | solution.py:339
  230.7 4.5 %reshape.61 = bf16[128,8192]{1,0:T(8,128)(2,1)} reshape(bf16[128,4,4,2,256]{4,3,2,1,0:T(2,128)(2,1)} %copy.13) | data formatting | bytes 4194304 | tf_op jit(solution)/shard_map/reshape | solution.py:339
  235.2 0.6 reshape.63
  236.0 5.9 %reshape.62 = bf16[192,8192]{1,0:T(8,128)(2,1)} reshape(bf16[16,192,512]{2,1,0:T(8,128)(2,1)} %get-tuple-element.8) | data formatting | bytes 6291456 | tf_op jit(solution)/shard_map/reshape | solution.py:341
  241.9 3.9 %fusion = f32[1,64,1024]{2,1,0:T(8,128)} fusion(bf16[192,1024]{1,0:T(8,128)(2,1)S(1)} %reshape.64, bf16[192,8192]{1,0:T(8,128)(2,1)} %reshape.62, bf16[1,8192,64]{1,2,0:T(8,128)(2,1)S(1)} %copy-done.6), kind=kOutput, calls=%fused_computation.4 | convolution fusion | flops 226570240 | bytes 4849664 | tf_op jit(solution)/shard_map/dot_general | solution.py:346
  245.8 3.9 %convolution_bitcast_fusion = f32[1,8192,64]{1,2,0:T(8,128)} fusion(bf16[192,8192]{1,0:T(8,128)(2,1)} %reshape.62, bf16[192,64]{1,0:T(8,128)(2,1)} %reshape.63), kind=kOutput, calls=%fused_computation.1 | convolution fusion | flops 201326592 | bytes 5267456 | tf_op jit(solution)/shard_map/dot_general | solution.py:349
  (13 shorter events, 0.2 us)
Async XLA Ops:
  0.6 11.3 %copy-start = (bf16[128,8192]{1,0:T(8,128)(2,1)S(1)}, bf16[128,8192]{1,0:T(8,128)(2,1)}, u32[]{:S(2)}) copy-start(bf16[128,8192]{1,0:T(8,128)(2,1)} %param.7) | copy-start | bytes 6291460
  20.4 1.0 copy-start.2
  21.4 0.9 copy-start.3
  22.4 0.8 copy-start.4
  23.2 1.2 copy-start.5
  218.8 1.3 copy-start.1
  235.9 6.0 %copy-start.6 = (bf16[1,8192,64]{1,2,0:T(8,128)(2,1)S(1)}, bf16[1,8192,64]{1,2,0:T(8,128)(2,1)}, u32[]{:S(2)}) copy-start(bf16[1,8192,64]{1,2,0:T(8,128)(2,1)} %param.12) | copy-start | bytes 3145732

commit v2 on v1

v2 whole, which is shorter than its diff:
```python
import functools

import jax
import jax.numpy as jnp
from jax import lax
from jax.experimental import pallas as pl
from jax.experimental.pallas import tpu as pltpu
from jax.sharding import PartitionSpec as P

adapter_scale = 2.0
MESH = pl.DeviceIdType.MESH
ROWS = 16
CHUNKS = 4
NT = (((1,), (1,)), ((), ()))
TN = (((0,), (0,)), ((), ()))


def ceil16(n):
    return -(-n // 16) * 16


def each(lo, hi, body):
    def step(k, c):
        body(k)
        return c

    lax.fori_loop(lo, hi, step, 0)


def exchange_kernel(
    G,
    S,
    N,
    cap,
    x_ref,
    dy_ref,
    w_ref,
    pt_ref,
    share_ref,
    place_x_ref,
    place_dy_ref,
    place_ref,
    hot_ref,
    q_ref,
    out_ref,
    down_ref,
    up_ref,
    dyr,
    rdy,
    lg,
    rlg,
    wsh,
    psh,
    share,
    dyp,
    tiles,
    osend,
    expand,
    xs,
    mid,
    hs,
    rows,
    hid,
    local_sem,
    dy_s,
    dy_r,
    lg_s,
    lg_r,
    wr_s,
    wl_s,
    w_r,
    pr_s,
    pl_s,
    p_r,
    pp_s,
    pp_r,
    h1_s,
    h1_r,
    h2_s,
    h2_r,
    b_s,
    b_r,
    t_s,
    t_r,
    o_s,
    o_r,
):
    bf16 = jnp.bfloat16
    f32 = jnp.float32
    PL = G * S
    L = N // S
    R = w_ref.shape[0]
    RG = R // G
    K = dy_ref.shape[1]
    rank = pt_ref.shape[0]
    C, _, RP, CD = xs.shape
    RQ = rows.shape[2]
    TL = tiles.shape[2]
    aligned = RG % 128 == 0
    pieces = L if aligned else 1
    me_g = lax.axis_index("groups")
    me = lax.axis_index("dp")
    me_z = me // S
    me_s = lax.rem(me, S)
    me_p = me_g * S + me_s

    def group_dev(k):
        return lax.rem(me + k, N)

    def plane_dev(k):
        p = lax.rem(me_p + k, PL)
        return (p // S, me_z * S + lax.rem(p, S)), p

    def line_dev(z):
        return (me_g, z * S + me_s)

    def rcopy(src, dst, ss, rs, dev):
        return pltpu.make_async_remote_copy(
            src_ref=src, dst_ref=dst, send_sem=ss, recv_sem=rs, device_id=dev, device_id_type=MESH
        )

    barrier = pltpu.get_barrier_semaphore()
    each(
        1,
        N,
        lambda k: pl.semaphore_signal(
            barrier, inc=1, device_id=(me_g, group_dev(k)), device_id_type=MESH
        ),
    )
    others = (G - 1) * S

    def greet(k):
        gg = lax.rem(me_g + 1 + k // S, G)
        pl.semaphore_signal(
            barrier, inc=1, device_id=(gg, me_z * S + lax.rem(k, S)), device_id_type=MESH
        )

    each(0, others, greet)
    dyr[...] = (
        jnp.dot(place_dy_ref[...], dy_ref[...], preferred_element_type=f32)
        .astype(bf16)
        .reshape(dyr.shape)
    )
    if aligned:
        for s in range(S):
            for z in range(L):
                start = pl.multiple_of((z * S + s) * R + me_g * RG, 128)
                share[s, :, z * RG : (z + 1) * RG] = pt_ref[:, pl.ds(start, RG)]
    else:
        share[...] = share_ref[...]
    pl.semaphore_wait(barrier, N - 1 + others)

    def dy_copy(k):
        d = group_dev(k)
        return rcopy(dyr.at[d], rdy.at[me], dy_s.at[k], dy_r.at[k], (me_g, d))

    each(1, N, lambda k: dy_copy(k).start())
    own_dy = pltpu.make_async_copy(dyr.at[me], rdy.at[me], local_sem.at[0])
    own_dy.start()

    w_part = w_ref.at[pl.ds(pl.multiple_of(me_g * RG, RG), RG)]
    own_w = pltpu.make_async_copy(w_part, wsh.at[me_z], local_sem.at[2])
    own_w.start()

    def pp_copy(k):
        s = lax.rem(me_s + k, S)
        return rcopy(
            share.at[s], psh.at[me_z, me_s], pp_s.at[k], pp_r.at[k], (me_g, me_z * S + s)
        )

    each(1, S, lambda k: pp_copy(k).start())
    own_p = pltpu.make_async_copy(share.at[me_s], psh.at[me_z, me_s], local_sem.at[3])
    own_p.start()

    def line_copies(buf, right_s, left_s, recv):
        def right(b):
            return rcopy(buf.at[b], buf.at[b], right_s.at[b], recv.at[b], line_dev(me_z + 1))

        def left(b):
            return rcopy(buf.at[b], buf.at[b], left_s.at[b], recv.at[b], line_dev(me_z - 1))

        return right, left

    def line_begin(right, left):
        @pl.when(me_z < L - 1)
        def _():
            right(me_z).start()

        @pl.when(me_z > 0)
        def _():
            left(me_z).start()

    def line_step(right, left, t):
        @pl.when(me_z - t >= 0)
        def _():
            right(me_z - t).wait_recv()

            @pl.when(me_z < L - 1)
            def _():
                right(me_z - t).start()

        @pl.when(me_z + t < L)
        def _():
            left(me_z + t).wait_recv()

            @pl.when(me_z > 0)
            def _():
                left(me_z + t).start()

    def line_end(right, left):
        def one(b):
            @pl.when(jnp.logical_and(b <= me_z, me_z < L - 1))
            def _():
                right(b).wait_send()

            @pl.when(jnp.logical_and(b >= me_z, me_z > 0))
            def _():
                left(b).wait_send()

        each(0, L, one)

    w_line = line_copies(wsh, wr_s, wl_s, w_r)
    p_line = line_copies(psh, pr_s, pl_s, p_r)

    def h1_copy(c, k):
        z = lax.rem(me_z + k, L)
        i = c * L + k
        return rcopy(xs.at[c, z], mid.at[c, me_z], h1_s.at[i], h1_r.at[i], line_dev(z))

    def own_mid(c):
        return pltpu.make_async_copy(xs.at[c, me_z], mid.at[c, me_z], local_sem.at[16 + c])

    def send_rows(c):
        start = pl.multiple_of(c * CD, CD)
        xs[c] = (
            jnp.dot(place_x_ref[...], x_ref[:, pl.ds(start, CD)], preferred_element_type=f32)
            .astype(bf16)
            .reshape(L, RP, CD)
        )
        each(1, L, lambda k: h1_copy(c, k).start())
        own_mid(c).start()

    def h2_copy(c, k):
        s = lax.rem(me_s + k, S)
        i = c * S + k
        return rcopy(
            hs.at[c, s], rows.at[c, me_s], h2_s.at[i], h2_r.at[i], (me_g, me_z * S + s)
        )

    def regroup(c):
        each(1, L, lambda k: h1_copy(c, k).wait_recv())
        own_mid(c).wait()

        def pick(s):
            q = lax.broadcasted_iota(jnp.int32, (RQ, L * RP), 0)
            j = lax.broadcasted_iota(jnp.int32, (RQ, L * RP), 1)
            hit = (j == (q // cap) * RP + s * cap + lax.rem(q, cap)) & (q < L * cap)
            sel = jnp.where(hit, 1.0, 0.0).astype(bf16)
            return jnp.dot(
                sel, mid[c].reshape(L * RP, CD), preferred_element_type=f32
            ).astype(bf16)

        def part(k):
            s = lax.rem(me_s + k, S)
            hs[c, s] = pick(s)
            h2_copy(c, k).start()

        each(1, S, part)
        rows[c, me_s] = pick(me_s)

    own_w.wait()
    line_begin(*w_line)
    send_rows(0)
    each(1, S, lambda k: pp_copy(k).wait_recv())
    own_p.wait()
    line_begin(*p_line)
    each(1, C, send_rows)

    def b_copy(k):
        dev, _ = plane_dev(k)
        return rcopy(dy_ref, dyp.at[me_p], b_s.at[k], b_r.at[k], dev)

    each(1, PL, lambda k: b_copy(k).start())
    own_b = pltpu.make_async_copy(dy_ref, dyp.at[me_p], local_sem.at[1])
    own_b.start()

    each(1, N, lambda k: dy_copy(k).wait_recv())
    own_dy.wait()
    value = adapter_scale * lax.dot_general(
        rdy[...].reshape(N * ROWS, K), q_ref[...], NT, preferred_element_type=f32
    )
    lg[...] = value.astype(bf16).reshape(lg.shape)

    def lg_copy(k):
        d = group_dev(k)
        return rcopy(lg.at[d], rlg.at[me], lg_s.at[k], lg_r.at[k], (me_g, d))

    each(1, N, lambda k: lg_copy(k).start())
    own_lg = pltpu.make_async_copy(lg.at[me], rlg.at[me], local_sem.at[4])
    own_lg.start()
    each(1, L, lambda t: line_step(*w_line, t))

    row = lax.broadcasted_iota(jnp.int32, (TL, N * rank), 0)
    col = lax.broadcasted_iota(jnp.int32, (TL, N * rank), 1)
    expand[0] = jnp.where(row == lax.rem(col, rank), 1.0, 0.0).astype(bf16)
    expand[1] = jnp.where(row - rank == col // rank, 1.0, 0.0).astype(bf16)

    each(1, N, lambda k: lg_copy(k).wait_recv())
    own_lg.wait()
    tokens = jnp.dot(
        place_ref[...], rlg[...].reshape(N * ROWS, TL), preferred_element_type=f32
    )
    tiles[me_p] = tokens.astype(bf16) + hot_ref[...]

    def t_copy(k):
        dev, _ = plane_dev(k)
        return rcopy(tiles.at[me_p], tiles.at[me_p], t_s.at[k], t_r.at[k], dev)

    each(1, PL, lambda k: t_copy(k).start())

    each(1, L, lambda t: line_step(*p_line, t))
    regroup(0)
    each(1, PL, lambda k: b_copy(k).wait_recv())
    own_b.wait()
    each(1, PL, lambda k: t_copy(k).wait_recv())

    def o_copy(k, i):
        dev, p = plane_dev(k)
        if not aligned:
            return rcopy(osend.at[p], out_ref.at[me_p], o_s.at[k], o_r.at[k], dev)
        start = pl.multiple_of((i * S + me_s) * R + me_g * RG, 128)
        return rcopy(
            osend.at[p, :, pl.ds(i * RG, RG)],
            out_ref.at[:, pl.ds(start, RG)],
            o_s.at[k * L + i],
            o_r.at[k * L + i],
            dev,
        )

    def own_out(i):
        if not aligned:
            return pltpu.make_async_copy(osend.at[me_p], out_ref.at[me_p], local_sem.at[8])
        start = pl.multiple_of((i * S + me_s) * R + me_g * RG, 128)
        return pltpu.make_async_copy(
            osend.at[me_p, :, pl.ds(i * RG, RG)],
            out_ref.at[:, pl.ds(start, RG)],
            local_sem.at[8 + i],
        )

    def block(k):
        p = lax.rem(me_p + k, PL)
        base = lax.dot_general(
            dyp[p], wsh[...].reshape(L * RG, K), NT, preferred_element_type=f32
        )
        tile = tiles[p]
        spread = jnp.dot(tile, expand[0], preferred_element_type=f32)
        chosen = jnp.dot(tile, expand[1], preferred_element_type=f32)
        masked = (spread * chosen).astype(bf16)
        term = jnp.dot(
            masked, psh[...].reshape(N * rank, L * RG), preferred_element_type=f32
        ).astype(bf16)
        osend[p] = (base + term.astype(f32)).astype(bf16)

    def block_and_send(k):
        block(k)
        for i in range(pieces):
            o_copy(k, i).start()

    each(1, PL, block_and_send)
    each(1, C, regroup)
    block(0)
    for i in range(pieces):
        own_out(i).start()

    q = lax.broadcasted_iota(jnp.int32, (S * RQ, N * ROWS), 0)
    j = lax.broadcasted_iota(jnp.int32, (S * RQ, N * ROWS), 1)
    inside = lax.rem(q, RQ)
    slot = ((inside // cap) * S + q // RQ) * ROWS + lax.rem(inside, cap)
    sel = jnp.where((j == slot) & (inside < L * cap), 1.0, 0.0).astype(bf16)
    lora = jnp.dot(sel, lg[...].reshape(N * ROWS, TL), preferred_element_type=f32).astype(bf16)
    grad = jnp.dot(sel, rdy[...].reshape(N * ROWS, K), preferred_element_type=f32).astype(bf16)

    hid[...] = jnp.zeros_like(hid)

    def finish(c):
        each(1, S, lambda k: h2_copy(c, k).wait_recv())
        start = pl.multiple_of(c * CD, CD)
        rc = rows[c].reshape(S * RQ, CD)
        hid[...] += lax.dot_general(
            rc, pt_ref[:, pl.ds(start, CD)], NT, preferred_element_type=f32
        )
        down_ref[:, pl.ds(start, CD)] = lax.dot_general(
            lora, rc, TN, preferred_element_type=f32
        )[:rank]

    each(0, C, finish)
    up_ref[...] = adapter_scale * lax.dot_general(
        hid[...].astype(bf16), grad, TN, preferred_element_type=f32
    )

    for i in range(pieces):
        each(1, PL, lambda k: o_copy(k, i).wait_recv())
        own_out(i).wait()
    each(1, N, lambda k: dy_copy(k).wait_send())
    each(1, N, lambda k: lg_copy(k).wait_send())
    each(1, S, lambda k: pp_copy(k).wait_send())
    for c in range(C):
        each(1, L, lambda k: h1_copy(c, k).wait_send())
        each(1, S, lambda k: h2_copy(c, k).wait_send())
    line_end(*w_line)
    line_end(*p_line)
    each(1, PL, lambda k: b_copy(k).wait_send())
    each(1, PL, lambda k: t_copy(k).wait_send())
    for i in range(pieces):
        each(1, PL, lambda k: o_copy(k, i).wait_send())


def per_device(
    G,
    inputs,
    output_gradient,
    token_adapter_index,
    owner_index_map,
    frozen_key_weight,
    down_panels,
    up_panels,
):
    N = lax.axis_size("dp")
    S = max(1, 8 // G)
    L = N // S
    PL = G * S
    T, D = inputs.shape
    K = output_gradient.shape[1]
    R = frozen_key_weight.shape[0]
    RG = R // G
    rank = down_panels.shape[2]
    cap = max(2, 3 * T // (2 * N))
    TL = -(-(rank + N) // 128) * 128
    RP = ceil16(S * cap)
    RQ = ceil16(L * cap)
    C = CHUNKS
    CD = D // C
    aligned = RG % 128 == 0
    pieces = L if aligned else 1
    bf16 = jnp.bfloat16
    f32 = jnp.float32

    index = token_adapter_index[:, 0]
    hot = index[:, None] == jnp.arange(N, dtype=jnp.int32)[None, :]
    before = jnp.arange(T)[:, None] > jnp.arange(T)[None, :]
    earlier = jnp.dot(before.astype(bf16), hot.astype(bf16), preferred_element_type=f32)
    turn = jnp.sum(jnp.where(hot, earlier, 0.0), axis=1).astype(jnp.int32)
    owner = jnp.sum(jnp.where(hot, owner_index_map[None, :], 0), axis=1)

    def numbers(n):
        return jnp.arange(n, dtype=jnp.int32)

    x_slot = (owner // S) * RP + (owner % S) * cap + turn
    place_x = (numbers(L * RP)[:, None] == x_slot[None, :]).astype(bf16)
    slot = owner * ROWS + turn
    place_dy = (numbers(N * ROWS)[:, None] == slot[None, :]).astype(bf16)
    place_t = (slot[:, None] == numbers(N * ROWS)[None, :]).astype(bf16)
    owner_hot = (owner[:, None] == numbers(TL)[None, :] - rank).astype(bf16)

    turned = down_panels[0].T
    if aligned:
        shares = turned
    else:
        group = lax.axis_index("groups")
        mine = lax.dynamic_index_in_dim(
            turned.reshape(rank, L, S, G, RG), group, 3, keepdims=False
        )
        shares = mine.transpose(2, 0, 1, 3).reshape(S, rank, L * RG)
    up_padded = jnp.pad(up_panels[0], ((0, TL - rank), (0, 0)))

    anyspace = pl.BlockSpec(memory_space=pl.ANY)
    vmem = pl.BlockSpec(memory_space=pltpu.VMEM)
    dma = pltpu.SemaphoreType.DMA
    out_shape = (T, D) if aligned else (PL, T, L * RG)
    outs, down, up = pl.pallas_call(
        functools.partial(exchange_kernel, G, S, N, cap),
        out_shape=(
            jax.ShapeDtypeStruct(out_shape, bf16),
            jax.ShapeDtypeStruct((rank, D), f32),
            jax.ShapeDtypeStruct((rank, K), f32),
        ),
        in_specs=[
            vmem,
            vmem,
            anyspace,
            vmem,
            anyspace if aligned else vmem,
            vmem,
            vmem,
            vmem,
            vmem,
            vmem,
        ],
        out_specs=[anyspace, vmem, vmem],
        scratch_shapes=[
            pltpu.VMEM((N, ROWS, K), bf16),
            pltpu.VMEM((N, ROWS, K), bf16),
            pltpu.VMEM((N, ROWS, TL), bf16),
            pltpu.VMEM((N, ROWS, TL), bf16),
            pltpu.VMEM((L, RG, K), bf16),
            pltpu.VMEM((L, S, rank, L * RG), bf16),
            pltpu.VMEM((S, rank, L * RG), bf16),
            pltpu.VMEM((PL, T, K), bf16),
            pltpu.VMEM((PL, T, TL), bf16),
            pltpu.VMEM((PL, T, L * RG), bf16),
            pltpu.VMEM((2, TL, N * rank), bf16),
            pltpu.VMEM((C, L, RP, CD), bf16),
            pltpu.VMEM((C, L, RP, CD), bf16),
            pltpu.VMEM((C, S, RQ, CD), bf16),
            pltpu.VMEM((C, S, RQ, CD), bf16),
            pltpu.VMEM((S * RQ, rank), f32),
            dma((16 + C,)),
        ]
        + [dma((N,))] * 4
        + [dma((L,))] * 6
        + [dma((S,))] * 2
        + [dma((C * L,))] * 2
        + [dma((C * S,))] * 2
        + [dma((PL,))] * 4
        + [dma((PL * pieces,))] * 2,
        compiler_params=pltpu.CompilerParams(
            collective_id=0, has_side_effects=True, vmem_limit_bytes=56 * 1024 * 1024
        ),
        cost_estimate=pl.CostEstimate(
            flops=4 * PL * T * L * RG * K, bytes_accessed=16 * 1024 * 1024, transcendentals=0
        ),
        name="exchange",
    )(
        inputs,
        output_gradient,
        frozen_key_weight,
        turned,
        shares,
        place_x,
        place_dy,
        place_t,
        owner_hot,
        up_padded,
    )

    if not aligned:
        outs = outs.reshape(G, S, T, L, RG).transpose(2, 3, 1, 0, 4).reshape(T, D)
    return (outs, down.T[None], up[None])


def solution(mesh):
    in_specs = (
        P(("groups", "dp"), None),
        P(("groups", "dp"), None),
        P(("groups", "dp"), None),
        P(),
        P("dp", None),
        P("dp", None, None),
        P("dp", None, None),
    )
    out_specs = (
        P(("groups", "dp"), None),
        P(("groups", "dp"), None, None),
        P(("groups", "dp"), None, None),
    )
    return jax.shard_map(
        functools.partial(per_device, mesh.shape["groups"]),
        mesh=mesh,
        in_specs=in_specs,
        out_specs=out_specs,
        check_vma=False,
    )
```

time: 253 us -> 232 us (0.917); the launches traced: 250 us -> 232 us
  local copies, waits for them, and re-layouts: 40.3 us -> 6.9 us
  Pallas kernels: 194 us -> 220 us
  matrix products: 12.5 us -> 0.88 us
    pallas_call x1, Pallas kernels: 194 us -> 220 us  [per_device(): pl.pallas_call(functools.partial(exchange_kernel, G, S, N, cap), out_shap...]
    reshape x7 -> x0, local copies, waits for them, and re-layouts: 22.6 us -> none  [the longest x2 8.96 us: per_device(): outs.reshape(G, S, T, L, RG).transpose(2, 3, 1, 0, 4).reshape(T, D)]
    dot_general x5 -> x1, matrix products: 12.5 us -> 0.88 us  [per_device(): jnp.dot(before.astype(bf16), hot.astype(bf16), preferred_element_type=f32)]
    transpose x1 -> x0, local copies, waits for them, and re-layouts: 6.14 us -> none  [per_device(): outs.reshape(G, S, T, L, RG).transpose(2, 3, 1, 0, 4).reshape(T, D)]
    dynamic_slice x2 -> x0, local copies, waits for them, and re-layouts: 2.71 us -> none  [per_device(): lax.dynamic_index_in_dim(panel.reshape(L, S, G, RG, rank), group, 2, keep...]
    another operation x1 -> x0, local copies, waits for them, and re-layouts: 2.61 us -> none  [per_device(): panel.reshape(L, S, G, RG, rank)]
    unnamed x14 -> x7, local copies, waits for them, and re-layouts: 5.3 us -> 5.27 us
where the time goes in v2:
time: 232 us
  Pallas kernels  220 us (95%)
  local copies, waits for them, and re-layouts  6.9 us (3%)
  other arithmetic  3.47 us (1%)
    pallas_call x1, Pallas kernels, per_device(): pl.pallas_call(functools.partial(exchange_kernel, G, S, N, cap), out_shap...  220 us
    unnamed x7, local copies, waits for them, and re-layouts  5.27 us

profile of v2, /device:TPU:1, one launch (start us, length us, event | category | flops | bytes accessed | tf_op | source)
XLA Modules:
  0.0 232.0 jit_solution(488065332923507875)
XLA Ops:
  0.6 0.8 select_reduce_fusion
  1.4 0.9 fusion
  2.3 0.7 compare_convert_fusion.hot_ref
  3.0 0.6 fusion.3.place_x_ref
  3.6 0.7 fusion.2.place_ref
  4.3 0.6 fusion.1.place_dy_ref
  5.0 1.6 pad.4.q_ref
  6.6 220.1 %exchange.1 = (bf16[128,8192]{1,0:T(8,128)(2,1)}, f32[64,8192]{1,0:T(8,128)}, f32[64,1024]{1,0:T(8,128)}) custom-call(bf16[128,8192]{1,0:T(8,128)(2,1)} %x_ref.1, bf16[128,1024]{1,0:T(8,128)(2,1)} %dy_ref.1, bf16[512,1024]{1,0:T(8,128)(2,1)} %w_ref.1, bf16[64,8192]{1,0:T(8,128)(2,1)} %bitcast.12, bf16[64,8192]{1,0:T(8,128)(2,1)} %bitcast.13, ...), custom_call_target="tpu_custom_call" | custom-call | flops 4294967296 | bytes 16777216 | tf_op jit(solution)/shard_map/exchange/pallas_call | solution.py:480
  226.7 0.0 copy-start
  226.7 3.2 %copy.13 = bf16[128,8192]{1,0:T(8,128)(2,1)} copy(bf16[128,8192]{1,0:T(8,128)(2,1)} %get-tuple-element.14) | data formatting | bytes 4194304
  230.0 0.0 copy-done
  230.0 0.0 copy-start.1
  230.0 1.3 copy.14
  231.3 0.0 copy-done.1
  231.3 0.7 copy.15
  (2 shorter events, 0.0 us)
Async XLA Ops:
  226.7 3.3 %copy-start = (f32[64,8192]{1,0:T(8,128)S(1)}, f32[64,8192]{1,0:T(8,128)}, u32[]{:S(2)}) copy-start(f32[64,8192]{1,0:T(8,128)} %get-tuple-element.7) | copy-start | bytes 6291460
  230.0 1.3 copy-start.1

commit v3 on v2

--- a/solution.py
+++ b/solution.py
@@ -55,7 +55,9 @@
     dyp,
     tiles,
     osend,
-    expand,
+    spread,
+    base,
+    acc,
     xs,
     mid,
     hs,
@@ -93,6 +95,7 @@
     RG = R // G
     K = dy_ref.shape[1]
     rank = pt_ref.shape[0]
+    T = dy_ref.shape[0]
     C, _, RP, CD = xs.shape
     RQ = rows.shape[2]
     TL = tiles.shape[2]
@@ -268,21 +271,19 @@
         each(1, S, part)
         rows[c, me_s] = pick(me_s)
 
+    def b_copy(k):
+        dev, _ = plane_dev(k)
+        return rcopy(dy_ref, dyp.at[me_p], b_s.at[k], b_r.at[k], dev)
+
+    each(1, PL, lambda k: b_copy(k).start())
+    own_b = pltpu.make_async_copy(dy_ref, dyp.at[me_p], local_sem.at[1])
+    own_b.start()
     own_w.wait()
     line_begin(*w_line)
-    send_rows(0)
     each(1, S, lambda k: pp_copy(k).wait_recv())
     own_p.wait()
     line_begin(*p_line)
-    each(1, C, send_rows)
-
-    def b_copy(k):
-        dev, _ = plane_dev(k)
-        return rcopy(dy_ref, dyp.at[me_p], b_s.at[k], b_r.at[k], dev)
-
-    each(1, PL, lambda k: b_copy(k).start())
-    own_b = pltpu.make_async_copy(dy_ref, dyp.at[me_p], local_sem.at[1])
-    own_b.start()
+    send_rows(0)
 
     each(1, N, lambda k: dy_copy(k).wait_recv())
     own_dy.wait()
@@ -298,12 +299,16 @@
     each(1, N, lambda k: lg_copy(k).start())
     own_lg = pltpu.make_async_copy(lg.at[me], rlg.at[me], local_sem.at[4])
     own_lg.start()
-    each(1, L, lambda t: line_step(*w_line, t))
-
-    row = lax.broadcasted_iota(jnp.int32, (TL, N * rank), 0)
-    col = lax.broadcasted_iota(jnp.int32, (TL, N * rank), 1)
-    expand[0] = jnp.where(row == lax.rem(col, rank), 1.0, 0.0).astype(bf16)
-    expand[1] = jnp.where(row - rank == col // rank, 1.0, 0.0).astype(bf16)
+
+    def base_piece(b):
+        if aligned:
+            base[:, pl.ds(pl.multiple_of(b * RG, RG), RG)] = lax.dot_general(
+                dyp[...].reshape(PL * T, K), wsh[b], NT, preferred_element_type=f32
+            )
+
+    each(1, PL, lambda k: b_copy(k).wait_recv())
+    own_b.wait()
+    base_piece(me_z)
 
     each(1, N, lambda k: lg_copy(k).wait_recv())
     own_lg.wait()
@@ -318,11 +323,68 @@
 
     each(1, PL, lambda k: t_copy(k).start())
 
-    each(1, L, lambda t: line_step(*p_line, t))
+    def column(rows_of, b):
+        row = lax.broadcasted_iota(jnp.int32, (TL, S * rank), 0)
+        col = lax.broadcasted_iota(jnp.int32, (TL, S * rank), 1)
+        hit = row == lax.rem(col, rank) if rows_of else row - rank == b * S + col // rank
+        return jnp.where(hit, 1.0, 0.0).astype(bf16)
+
+    def lora_piece(b):
+        chosen = jnp.dot(
+            tiles[...].reshape(PL * T, TL), column(False, b), preferred_element_type=f32
+        )
+        masked = (spread[...].astype(f32) * chosen).astype(bf16)
+        for i in range(0, L * RG, 256):
+            acc[:, i : i + 256] += jnp.dot(
+                masked,
+                psh[b].reshape(S * rank, L * RG)[:, i : i + 256],
+                preferred_element_type=f32,
+            )
+
+    def line_use(t):
+        @pl.when(me_z - t >= 0)
+        def _():
+            base_piece(me_z - t)
+            lora_piece(me_z - t)
+
+        @pl.when(me_z + t < L)
+        def _():
+            base_piece(me_z + t)
+            lora_piece(me_z + t)
+
+    acc[...] = jnp.zeros_like(acc)
+    line_step(*w_line, 1)
+    line_step(*p_line, 1)
+    send_rows(1)
+    each(1, PL, lambda k: t_copy(k).wait_recv())
+    spread[...] = jnp.dot(
+        tiles[...].reshape(PL * T, TL), column(True, 0), preferred_element_type=f32
+    ).astype(bf16)
+    lora_piece(me_z)
+    line_use(1)
+    if L > 2:
+        line_step(*w_line, 2)
+        line_step(*p_line, 2)
+        send_rows(2)
+        line_use(2)
+    else:
+        send_rows(2)
+
+    def later(t):
+        line_step(*w_line, t)
+        line_step(*p_line, t)
+        line_use(t)
+
+    send_rows(3)
     regroup(0)
-    each(1, PL, lambda k: b_copy(k).wait_recv())
-    own_b.wait()
-    each(1, PL, lambda k: t_copy(k).wait_recv())
+    each(3, L, later)
+    if not aligned:
+        base[...] = lax.dot_general(
+            dyp[...].reshape(PL * T, K),
+            wsh[...].reshape(L * RG, K),
+            NT,
+            preferred_element_type=f32,
+        )
 
     def o_copy(k, i):
         dev, p = plane_dev(k)
@@ -349,17 +411,9 @@
 
     def block(k):
         p = lax.rem(me_p + k, PL)
-        base = lax.dot_general(
-            dyp[p], wsh[...].reshape(L * RG, K), NT, preferred_element_type=f32
-        )
-        tile = tiles[p]
-        spread = jnp.dot(tile, expand[0], preferred_element_type=f32)
-        chosen = jnp.dot(tile, expand[1], preferred_element_type=f32)
-        masked = (spread * chosen).astype(bf16)
-        term = jnp.dot(
-            masked, psh[...].reshape(N * rank, L * RG), preferred_element_type=f32
-        ).astype(bf16)
-        osend[p] = (base + term.astype(f32)).astype(bf16)
+        at = pl.ds(pl.multiple_of(p * T, T), T)
+        term = acc[at].astype(bf16).astype(f32)
+        osend[p] = (base[at] + term).astype(bf16)
 
     def block_and_send(k):
         block(k)
@@ -367,7 +421,6 @@
             o_copy(k, i).start()
 
     each(1, PL, block_and_send)
-    each(1, C, regroup)
     block(0)
     for i in range(pieces):
         own_out(i).start()
@@ -381,6 +434,7 @@
     grad = jnp.dot(sel, rdy[...].reshape(N * ROWS, K), preferred_element_type=f32).astype(bf16)
 
     hid[...] = jnp.zeros_like(hid)
+    each(1, C, regroup)
 
     def finish(c):
         each(1, S, lambda k: h2_copy(c, k).wait_recv())
@@ -508,7 +562,9 @@
             pltpu.VMEM((PL, T, K), bf16),
             pltpu.VMEM((PL, T, TL), bf16),
             pltpu.VMEM((PL, T, L * RG), bf16),
-            pltpu.VMEM((2, TL, N * rank), bf16),
+            pltpu.VMEM((PL * T, S * rank), bf16),
+            pltpu.VMEM((PL * T, L * RG), f32),
+            pltpu.VMEM((PL * T, L * RG), f32),
             pltpu.VMEM((C, L, RP, CD), bf16),
             pltpu.VMEM((C, L, RP, CD), bf16),
             pltpu.VMEM((C, S, RQ, CD), bf16),
@@ -524,7 +580,7 @@
         + [dma((PL,))] * 4
         + [dma((PL * pieces,))] * 2,
         compiler_params=pltpu.CompilerParams(
-            collective_id=0, has_side_effects=True, vmem_limit_bytes=56 * 1024 * 1024
+            collective_id=0, has_side_effects=True, vmem_limit_bytes=58 * 1024 * 1024
         ),
         cost_estimate=pl.CostEstimate(
             flops=4 * PL * T * L * RG * K, bytes_accessed=16 * 1024 * 1024, transcendentals=0

time: 232 us -> 208 us (0.90)
  Pallas kernels: 220 us -> 196 us
    pallas_call x1, Pallas kernels: 220 us -> 196 us  [per_device(): pl.pallas_call(functools.partial(exchange_kernel, G, S, N, cap), out_shap...]
where the time goes in v3:
time: 208 us
  Pallas kernels  196 us (94%)
  local copies, waits for them, and re-layouts  6.9 us (3%)
  other arithmetic  3.47 us (2%)
    pallas_call x1, Pallas kernels, per_device(): pl.pallas_call(functools.partial(exchange_kernel, G, S, N, cap), out_shap...  196 us
    unnamed x7, local copies, waits for them, and re-layouts  5.27 us

profile of v3, /device:TPU:1, one launch (start us, length us, event | category | flops | bytes accessed | tf_op | source)
XLA Modules:
  0.0 207.6 jit_solution(16631910093527467888)
XLA Ops:
  0.6 0.8 select_reduce_fusion
  1.4 0.9 fusion
  2.3 0.7 compare_convert_fusion.hot_ref
  3.0 0.6 fusion.3.place_x_ref
  3.6 0.7 fusion.2.place_ref
  4.3 0.6 fusion.1.place_dy_ref
  5.0 1.6 pad.4.q_ref
  6.6 195.6 %exchange.1 = (bf16[128,8192]{1,0:T(8,128)(2,1)}, f32[64,8192]{1,0:T(8,128)}, f32[64,1024]{1,0:T(8,128)}) custom-call(bf16[128,8192]{1,0:T(8,128)(2,1)} %x_ref.1, bf16[128,1024]{1,0:T(8,128)(2,1)} %dy_ref.1, bf16[512,1024]{1,0:T(8,128)(2,1)} %w_ref.1, bf16[64,8192]{1,0:T(8,128)(2,1)} %bitcast.12, bf16[64,8192]{1,0:T(8,128)(2,1)} %bitcast.13, ...), custom_call_target="tpu_custom_call" | custom-call | flops 4294967296 | bytes 16777216 | tf_op jit(solution)/shard_map/exchange/pallas_call | solution.py:534
  202.3 0.0 copy-start
  202.3 3.2 %copy.13 = bf16[128,8192]{1,0:T(8,128)(2,1)} copy(bf16[128,8192]{1,0:T(8,128)(2,1)} %get-tuple-element.14) | data formatting | bytes 4194304
  205.5 0.0 copy-done
  205.5 0.0 copy-start.1
  205.5 1.3 copy.14
  206.8 0.0 copy-done.1
  206.8 0.7 copy.15
  (2 shorter events, 0.0 us)
Async XLA Ops:
  202.3 3.3 %copy-start = (f32[64,8192]{1,0:T(8,128)S(1)}, f32[64,8192]{1,0:T(8,128)}, u32[]{:S(2)}) copy-start(f32[64,8192]{1,0:T(8,128)} %get-tuple-element.7) | copy-start | bytes 6291460
  205.5 1.3 copy-start.1

commit v4 on v3

--- a/solution.py
+++ b/solution.py
@@ -306,9 +306,9 @@
                 dyp[...].reshape(PL * T, K), wsh[b], NT, preferred_element_type=f32
             )
 
-    each(1, PL, lambda k: b_copy(k).wait_recv())
-    own_b.wait()
-    base_piece(me_z)
+    send_rows(1)
+    line_step(*w_line, 1)
+    line_step(*p_line, 1)
 
     each(1, N, lambda k: lg_copy(k).wait_recv())
     own_lg.wait()
@@ -352,10 +352,15 @@
             base_piece(me_z + t)
             lora_piece(me_z + t)
 
+    send_rows(2)
     acc[...] = jnp.zeros_like(acc)
-    line_step(*w_line, 1)
-    line_step(*p_line, 1)
-    send_rows(1)
+    each(1, PL, lambda k: b_copy(k).wait_recv())
+    own_b.wait()
+    base_piece(me_z)
+    if L > 2:
+        line_step(*w_line, 2)
+        line_step(*p_line, 2)
+    send_rows(3)
     each(1, PL, lambda k: t_copy(k).wait_recv())
     spread[...] = jnp.dot(
         tiles[...].reshape(PL * T, TL), column(True, 0), preferred_element_type=f32
@@ -363,19 +368,13 @@
     lora_piece(me_z)
     line_use(1)
     if L > 2:
-        line_step(*w_line, 2)
-        line_step(*p_line, 2)
-        send_rows(2)
         line_use(2)
-    else:
-        send_rows(2)
 
     def later(t):
         line_step(*w_line, t)
         line_step(*p_line, t)
         line_use(t)
 
-    send_rows(3)
     regroup(0)
     each(3, L, later)
     if not aligned:

time: 208 us -> 207 us (level)
  no operation moved by 1% of the time
where the time goes in v4:
time: 207 us; the launch traced here: 206 us
  Pallas kernels  195 us (94%)
  local copies, waits for them, and re-layouts  6.9 us (3%)
  other arithmetic  3.47 us (2%)
    pallas_call x1, Pallas kernels, per_device(): pl.pallas_call(functools.partial(exchange_kernel, G, S, N, cap), out_shap...  195 us
    unnamed x7, local copies, waits for them, and re-layouts  5.27 us

profile of v4, /device:TPU:1, one launch (start us, length us, event | category | flops | bytes accessed | tf_op | source)
XLA Modules:
  0.0 206.5 jit_solution(1835266170182347022)
XLA Ops:
  0.6 0.8 select_reduce_fusion
  1.4 0.9 fusion
  2.3 0.7 compare_convert_fusion.hot_ref
  3.0 0.6 fusion.3.place_x_ref
  3.6 0.7 fusion.2.place_ref
  4.3 0.6 fusion.1.place_dy_ref
  5.0 1.6 pad.4.q_ref
  6.6 194.5 %exchange.1 = (bf16[128,8192]{1,0:T(8,128)(2,1)}, f32[64,8192]{1,0:T(8,128)}, f32[64,1024]{1,0:T(8,128)}) custom-call(bf16[128,8192]{1,0:T(8,128)(2,1)} %x_ref.1, bf16[128,1024]{1,0:T(8,128)(2,1)} %dy_ref.1, bf16[512,1024]{1,0:T(8,128)(2,1)} %w_ref.1, bf16[64,8192]{1,0:T(8,128)(2,1)} %bitcast.12, bf16[64,8192]{1,0:T(8,128)(2,1)} %bitcast.13, ...), custom_call_target="tpu_custom_call" | custom-call | flops 4294967296 | bytes 16777216 | tf_op jit(solution)/shard_map/exchange/pallas_call | solution.py:533
  201.2 0.0 copy-start
  201.2 3.2 %copy.13 = bf16[128,8192]{1,0:T(8,128)(2,1)} copy(bf16[128,8192]{1,0:T(8,128)(2,1)} %get-tuple-element.14) | data formatting | bytes 4194304
  204.4 0.0 copy-done
  204.4 0.0 copy-start.1
  204.4 1.3 copy.14
  205.7 0.0 copy-done.1
  205.7 0.7 copy.15
  (2 shorter events, 0.0 us)
Async XLA Ops:
  201.2 3.3 %copy-start = (f32[64,8192]{1,0:T(8,128)S(1)}, f32[64,8192]{1,0:T(8,128)}, u32[]{:S(2)}) copy-start(f32[64,8192]{1,0:T(8,128)} %get-tuple-element.7) | copy-start | bytes 6291460
  204.4 1.3 copy-start.1
